TPU v7x, 256 devices: a whole 4x4x8 slice. The times are simulated.
256 devices in a mesh: dp: 32 (over z_hi, y, core), tensor: 8 (over x, z_lo).
Axes of the slice: x: 4, y: 4, z: 8 (z_hi: 4, z_lo: 2; z = z_hi * 2 + z_lo), core: 2. Of those that a mesh axis runs over, the one named last changes fastest.
Arguments:
- gate_pre: bfloat16 [8192, 14336], P('dp', 'tensor'), may hold values from -6 to 6
- up_pre: bfloat16 [8192, 14336], P('dp', 'tensor'), may hold values from -6 to 6
- cotangent: bfloat16 [8192, 4096], P(('dp', 'tensor')), may hold values from -24 to 24
- w_prev: bfloat16 [14336, 4096], P('tensor', 'dp'), may hold values from -0.09375 to 0.09375
- param_next: float32 [14336, 4096], P('tensor', 'dp'), may hold values from -0.75 to 0.75
- grad_next: float32 [14336, 4096], P('tensor', 'dp'), may hold values from -6 to 6
- moment_one: bfloat16 [14336, 4096], P('tensor', 'dp'), may hold values from -4 to 4
- moment_two: bfloat16 [14336, 4096], P('tensor', 'dp'), may hold values from 0.0099487305 to 1
Outputs:
- gate_grad: bfloat16 [8192, 14336], P('dp', 'tensor')
- up_grad: bfloat16 [8192, 14336], P('dp', 'tensor')
- grad_prev: float32 [14336, 4096], P('tensor', 'dp')
- param_new: float32 [14336, 4096], P('tensor', 'dp')
- moment_one_new: bfloat16 [14336, 4096], P('tensor', 'dp')
- moment_two_new: bfloat16 [14336, 4096], P('tensor', 'dp')
- adam_step: float32 [14336, 4096], P('tensor', 'dp')
All inputs are finite; a program needn't handle non-finite values.
Results may differ from a plain program's by a relative error of at most 0.02.
Values may be sent and summed in bfloat16 or wider, within the bound.
A program may use at most 128 MiB of HBM per device.

v0:
```python
import jax
import jax.numpy as jnp
from jax import lax
from jax.sharding import PartitionSpec as P

STEP = 10


beta_first = 0.9
beta_second = 0.95
epsilon = 1e-08
decay_rate = 0.1
learn_rate = 0.0003
unscale = 1.0 / 32.0


def body(gate_pre, up_pre, cotangent, w_prev, param_next, grad_next, moment_one, moment_two):
    cotangent_all = lax.all_gather(cotangent, "tensor", axis=0, tiled=True)
    gate_vals = gate_pre.astype(jnp.float32)
    up_vals = up_pre.astype(jnp.float32)
    gate_sig = jax.nn.sigmoid(gate_vals)
    gate_act = gate_vals * gate_sig
    hidden = (gate_act * up_vals).astype(jnp.bfloat16)
    full_term = lax.dot_general(
        cotangent_all, hidden, (((0,), (0,)), ((), ())), preferred_element_type=jnp.float32
    )
    reduced = lax.psum_scatter(
        full_term.astype(jnp.bfloat16), "dp", scatter_dimension=0, tiled=True
    ).astype(jnp.float32)
    grad_prev = (reduced * unscale).T
    weight_full = lax.all_gather(w_prev, "dp", axis=1, tiled=True)
    hidden_grad = lax.dot_general(
        cotangent_all, weight_full, (((1,), (1,)), ((), ())), preferred_element_type=jnp.float32
    )
    up_grad = (hidden_grad * gate_act).astype(jnp.bfloat16)
    gate_grad = (hidden_grad * up_vals * gate_sig * (1.0 + gate_vals * (1.0 - gate_sig))).astype(
        jnp.bfloat16
    )
    moment_one_f = beta_first * moment_one.astype(jnp.float32) + (1.0 - beta_first) * grad_next
    moment_two_f = (
        beta_second * moment_two.astype(jnp.float32) + (1.0 - beta_second) * grad_next * grad_next
    )
    first_fix = 1.0 - beta_first**STEP
    second_fix = 1.0 - beta_second**STEP
    adam_step = (
        moment_one_f / first_fix / (jnp.sqrt(moment_two_f / second_fix) + epsilon)
        + decay_rate * param_next
    )
    param_new = param_next - learn_rate * adam_step
    return (
        gate_grad,
        up_grad,
        grad_prev,
        param_new,
        moment_one_f.astype(jnp.bfloat16),
        moment_two_f.astype(jnp.bfloat16),
        adam_step,
    )


def solution(mesh):
    in_specs = (
        P("dp", "tensor"),
        P("dp", "tensor"),
        P(("dp", "tensor"), None),
        P("tensor", "dp"),
        P("tensor", "dp"),
        P("tensor", "dp"),
        P("tensor", "dp"),
        P("tensor", "dp"),
    )
    out_specs = (
        P("dp", "tensor"),
        P("dp", "tensor"),
        P("tensor", "dp"),
        P("tensor", "dp"),
        P("tensor", "dp"),
        P("tensor", "dp"),
        P("tensor", "dp"),
    )
    return jax.shard_map(body, mesh=mesh, in_specs=in_specs, out_specs=out_specs, check_vma=False)
```

profile of v0, /device:TPU:1, one launch (start us, length us, event | category | flops | bytes accessed | tf_op | source)
XLA Modules:
  0.0 394.2 jit_solution(3735431573443063802)
XLA Ops:
  7.2 0.0 all-gather.3.cloned.1.call-start
  7.2 0.7 all-gather.3.cloned.1.call-update
  7.9 0.0 reduce-scatter.4.cloned.1.call-start
  7.9 60.2 %all-gather.3.cloned.1.call-done = bf16[256,4096]{1,0:T(8,128)(2,1)} async-done(((bf16[32,4096]{1,0:T(8,128)(2,1)}), bf16[256,4096]{1,0:T(8,128)(2,1)}) %all-gather.3.cloned.1.call-update) | async-done | bytes 2097168 | tf_op jit(solution)/shard_map/all_gather | solution.py:18
  68.1 11.6 %fusion = bf16[4096,1792]{0,1:T(8,128)(2,1)} fusion(bf16[256,4096]{1,0:T(8,128)(2,1)} %all-gather.3.cloned.1.call-done, bf16[256,1792]{1,0:T(8,128)(2,1)} %param.9, bf16[256,1792]{1,0:T(8,128)(2,1)} %param.8), kind=kOutput, calls=%fused_computation.1 | convolution fusion | flops 3769106432 | bytes 18612224 | tf_op jit(solution)/shard_map/dot_general | solution.py:24
  79.7 18.7 %copy.15 = bf16[4096,1792]{1,0:T(8,128)(2,1)} copy(bf16[4096,1792]{0,1:T(8,128)(2,1)} %fusion) | data formatting | bytes 29360128
  98.4 0.0 copy-start
  98.4 0.0 copy-start.1
  98.4 0.0 copy-start.2
  98.5 0.0 copy-start.3
  98.5 0.0 reduce-scatter.4.cloned.1.call-update
  98.5 0.0 all-gather.5.cloned.1.call-start
  98.5 0.7 all-gather.5.cloned.1.call-update
  99.2 0.4 copy-done
  99.6 0.3 copy-done.1
  99.9 0.1 copy-done.2
  100.0 0.1 copy-done.3
  100.2 2.6 multiply_subtract_fusion
  102.7 0.0 copy-start.4
  102.7 146.8 %reduce-scatter.4.cloned.1.call-done = bf16[128,1792]{1,0:T(8,128)(2,1)} async-done(((bf16[4096,1792]{1,0:T(8,128)(2,1)}), bf16[128,1792]{1,0:T(8,128)(2,1)}) %reduce-scatter.4.cloned.1.call-update) | async-done | bytes 458768
  249.5 1.3 copy.16
  250.8 1.0 multiply_bitcast_fusion
  251.8 119.3 %all-gather.5.cloned.1.call-done = bf16[1792,4096]{1,0:T(8,128)(2,1)} async-done(((bf16[1792,128]{1,0:T(8,128)(2,1)}), bf16[1792,4096]{1,0:T(8,128)(2,1)}) %all-gather.5.cloned.1.call-update) | async-done | bytes 14680080 | tf_op jit(solution)/shard_map/all_gather | solution.py:31
  371.1 0.0 copy-done.4
  371.1 16.6 %multiply_convert_fusion = (bf16[256,1792]{1,0:T(8,128)(2,1)}, bf16[256,1792]{1,0:T(8,128)(2,1)}) fusion(bf16[256,1792]{1,0:T(8,128)(2,1)} %param.8, bf16[256,1792]{1,0:T(8,128)(2,1)} %param.9, bf16[256,4096]{1,0:T(8,128)(2,1)S(1)} %copy-done.4, bf16[1792,4096]{1,0:T(8,128)(2,1)} %all-gather.5.cloned.1.call-done), kind=kOutput, calls=%fused_computation.15 | convolution fusion | flops 3764977664 | bytes 20447232 | tf_op jit(solution)/shard_map/dot_general | solution.py:32
Async XLA Ops:
  7.2 60.9 %all-gather.3.cloned.1.call-start = ((), (), s32[]{:S(2)}) async-start(), calls=%async_computation.1 | async-start | bytes 2359296 | tf_op jit(solution)/shard_map/all_gather | solution.py:18
  7.9 241.6 %reduce-scatter.4.cloned.1.call-start = ((), (), s32[]{:S(2)}) async-start(), calls=%async_computation.3 | async-start | bytes 15138816
  98.4 1.2 copy-start
  98.4 1.5 copy-start.1
  98.4 1.6 copy-start.2
  98.5 1.7 copy-start.3
  98.5 272.6 %all-gather.5.cloned.1.call-start = ((), (), s32[]{:S(2)}) async-start(), calls=%async_computation.2 | async-start | bytes 15138816 | tf_op jit(solution)/shard_map/all_gather | solution.py:31
  102.7 268.4 %copy-start.4 = (bf16[256,4096]{1,0:T(8,128)(2,1)S(1)}, bf16[256,4096]{1,0:T(8,128)(2,1)}, u32[]{:S(2)}) copy-start(bf16[256,4096]{1,0:T(8,128)(2,1)} %all-gather.3.cloned.1.call-done) | copy-start | bytes 6291460
Sparse Core Ops, SparseCore 0:
  9.8 58.2 all-gather.2
  98.6 150.8 reduce-scatter.3
  252.3 118.7 all-gather.4
where the time goes:
time: 395 us; the launch traced here: 394 us
  waiting for transfers between devices  328 us (83%)
  matrix products  28.2 us (7%)
  local copies, waits for them, and re-layouts  20.9 us (5%)
  between operations  13.8 us (3%)
    unnamed x4, waiting for transfers between devices  148 us
    all_gather x1, waiting for transfers between devices, body(): weight_full = lax.all_gather(w_prev, 'dp', axis=1, tiled=True)  119 us
    all_gather x1, waiting for transfers between devices, body(): cotangent_all = lax.all_gather(cotangent, 'tensor', axis=0, tiled=True)  60.2 us
    unnamed x12, local copies, waits for them, and re-layouts  20.9 us
    dot_general x1, matrix products, body(): lax.dot_general(cotangent_all, weight_full, (((1,), (1,)), ((), ())), pre...  16.6 us
    dot_general x1, matrix products, body(): lax.dot_general(cotangent_all, hidden, (((0,), (0,)), ((), ())), preferre...  11.6 us
  transfers between devices with their start and end apart: 3, of which 3 were waited for; matrix products, arithmetic and copies ran while one was open for 1% of the time, Pallas kernels for 0%

commit v1 on v0

v1 whole, which is shorter than its diff:
```python
import jax
import jax.numpy as jnp
from jax import lax
from jax.experimental import pallas as pl
from jax.experimental.pallas import tpu as pltpu
from jax.sharding import PartitionSpec as P

STEP = 10


beta_first = 0.9
beta_second = 0.95
epsilon = 1e-08
decay_rate = 0.1
learn_rate = 0.0003
unscale = 1.0 / 32.0

MESH = pl.DeviceIdType.MESH
F32, BF16 = jnp.float32, jnp.bfloat16

TOK, HID, QUARTER, WIDE, CHUNK, SHARD = 256, 1792, 448, 512, 1024, 128
ORD = (2, 1, 3, 0)
SLOT = {o: k for k, o in enumerate(ORD)}
STEPS = [(k, j) for k in range(3) for j in (0, 1, 3, 2)] + [(3, j) for j in (2, 3, 1, 0)]
RIGHT = (0, 3)


def back(j):
    return (4 - j) % 4


def kernel(
    gate_ref, up_ref, cot_ref, w_ref, gg_ref, ug_ref, gp_ref,
    gate_v, up_v, act_v, fac_v, hidh, hidt, cot_v, w_v, px_s, px_r, pown, ps, gr,
    hg_acc, hg_s, hg_r, gg_v, ug_v, gp_v,
    ld, zl_s, zl_r, y_s, y_r, xr_s, xl_s, fl_r, fr_r, xf_s, xf_r, w_s, w_r, wc_s, wc_r,
    h_s, h_r, g_s, g_r, pc_s, pc_r, p_s, p_r, out_s,
):
    dp, tn = lax.axis_index("dp"), lax.axis_index("tensor")
    c, y, zh = dp % 2, (dp // 2) % 4, dp // 8
    x, zl = tn // 2, tn % 2

    def plane(o, j):
        return ((((zh + o) % 4) * 4 + (y + j) % 4) * 2 + c, tn)

    other_core = (dp + 1 - 2 * c, tn)
    other_zl = (dp, tn + 1 - 2 * zl)
    right = (dp, ((x + 1) % 4) * 2 + zl)
    left = (dp, ((x + 3) % 4) * 2 + zl)

    def remote(src, dst, send, recv, device):
        return pltpu.make_async_remote_copy(
            src_ref=src, dst_ref=dst, send_sem=send, recv_sem=recv,
            device_id=device, device_id_type=MESH,
        )

    sent = []

    def start(copy):
        copy.start()
        sent.append(copy)

    def arrived(ref, recv, send):
        remote(ref, ref, send, recv, other_core).wait_recv()

    def chunk_cols(k):
        return pl.ds(pl.multiple_of(((zh + ORD[k]) % 4) * CHUNK, CHUNK), CHUNK)

    def rows_at(j, xx, n=64, extra=0):
        return pl.ds(pl.multiple_of(j * TOK + xx * 64 + extra, 32), n)

    peers = [plane(o, j) for o in range(4) for j in range(4) if (o, j) != (0, 0)]
    peers += [other_core, other_zl, right, left]
    barrier = pltpu.get_barrier_semaphore()
    for peer in peers:
        pl.semaphore_signal(barrier, inc=1, device_id=peer, device_id_type=MESH)

    own_rows = rows_at(0, x, 32, zl * 32)
    loads = []
    for k in range(4):
        loads.append(pltpu.make_async_copy(
            cot_ref.at[:, chunk_cols(k)], cot_v.at[k, own_rows], ld.at[k]))
    loads.append(pltpu.make_async_copy(gate_ref, gate_v, ld.at[4]))
    loads.append(pltpu.make_async_copy(up_ref, up_v, ld.at[5]))

    def quarter_rows(j):
        return pl.ds(pl.multiple_of(((y + j) % 4) * QUARTER, QUARTER), QUARTER)

    def w_rows(j):
        return pl.ds(pl.multiple_of(((y + j) % 2) * 64, 64), QUARTER)

    def w_cols(j, cc):
        return pl.ds(pl.multiple_of((((y + j) % 4) * 2 + cc) * SHARD, SHARD), SHARD)

    loads.append(pltpu.make_async_copy(
        w_ref.at[quarter_rows(0)], w_v.at[3, w_rows(0), w_cols(0, c)], ld.at[6]))
    for load in loads:
        load.start()
    pad = pl.ds(pl.multiple_of((1 - y % 2) * QUARTER, 64), 64)
    for k in range(4):
        w_v[k, pad, :] = jnp.zeros((64, CHUNK), BF16)
    pl.semaphore_wait(barrier, len(peers))

    for k in range(4):
        start(remote(cot_ref.at[:, chunk_cols(k)], cot_v.at[k, own_rows],
                     zl_s.at[k], zl_r.at[k], other_zl))
    partner_rows = rows_at(0, x, 32, (1 - zl) * 32)

    def y_sends(k):
        loads[k].wait()
        arrived(cot_v.at[k, partner_rows], zl_r.at[k], zl_s.at[k])
        for j in ((2, 3, 1) if k == 3 else (1, 3, 2)):
            start(remote(cot_v.at[k, rows_at(0, x)], cot_v.at[k, rows_at(back(j), x)],
                         y_s.at[k, j], y_r.at[k, back(j)], plane(0, j)))

    def w_sends():
        for o, j in [(1, 0), (3, 0), (1, 1), (3, 1), (1, 3), (3, 3), (1, 2), (3, 2),
                     (0, 1), (0, 3), (0, 2)]:
            k = SLOT[back(o)]
            start(remote(w_ref.at[quarter_rows(j)], w_v.at[k, w_rows(j), w_cols(0, c)],
                         w_s.at[k, back(j)], w_r.at[k, back(j)], plane(o, j)))

    def w_block(k, j, cc):
        return w_v.at[k, w_rows(0), w_cols(j, cc)]

    def w_arrived(k, j):
        if (k, j) == (3, 0):
            loads[6].wait()
        else:
            arrived(w_block(k, j, c), w_r.at[k, j], w_s.at[k, j])
        start(remote(w_block(k, j, c), w_block(k, j, c), wc_s.at[k, j], wc_r.at[k, j], other_core))

    def w_near():
        for k, o, blocks in ((SLOT[1], 3, (0, 1)), (SLOT[3], 1, (2, 3))):
            for j in range(4):
                w_arrived(k, j)
                if j in blocks:
                    start(remote(w_block(k, j, c), w_block(0, j, c),
                                 w_s.at[0, j], w_r.at[0, j], plane(o, 0)))
        for j in range(4):
            w_arrived(3, j)

    def w_far():
        for j in range(4):
            w_arrived(0, j)

    def w_other(k):
        for j in range(4):
            arrived(w_block(k, j, 1 - c), wc_r.at[k, j], wc_s.at[k, j])

    def home():
        loads[4].wait()
        loads[5].wait()

        def block(f, _):
            cols = pl.ds(pl.multiple_of(f * 128, 128), 128)
            g = gate_v[:, cols].astype(F32)
            u = up_v[:, cols].astype(F32)
            s = jax.nn.sigmoid(g)
            act = g * s
            act_v[:, cols] = act
            fac_v[:, cols] = u * s * (1.0 + g * (1.0 - s))
            hidh[cols, :] = (act * u).T.astype(BF16)
            return 0

        lax.fori_loop(0, HID // 128, block, 0)

    def hidden_sends():
        for j in (2, 1, 3):
            start(remote(hidh.at[quarter_rows(j)], hidt.at[:, pl.ds(back(j) * TOK, TOK)],
                         h_s.at[j], h_r.at[back(j)], plane(0, j)))
        hidt[:, 0:TOK] = hidh[quarter_rows(0), :]

    def hidden_arrived():
        for j in (1, 3, 2):
            arrived(hidt.at[:, pl.ds(j * TOK, TOK)], h_r.at[j], h_s.at[j])

    def term(k):
        def tile(j, _):
            cols = pl.ds(pl.multiple_of(((y + j) % 4) * 256, 256), 256)
            part = jnp.dot(hidt[...], cot_v[k, :, cols], preferred_element_type=F32)
            low, high = part[:, :SHARD], part[:, SHARD:]
            pown[j] = jnp.where(c == 0, low, high)
            px_s[k, j] = jnp.where(c == 0, high, low).astype(BF16)
            return 0

        lax.fori_loop(0, 4, tile, 0)
        start(remote(px_s.at[k], px_r.at[k], pc_s.at[k], pc_r.at[k], other_core))

    def term_sends(k):
        arrived(px_r.at[k], pc_r.at[k], pc_s.at[k])
        for j in (2, 1, 3, 0):
            total = (pown[j] + px_r[k, j].astype(F32)).astype(BF16)
            if (k, j) == (3, 0):
                gr[3, 0] = total
            else:
                ps[k, j] = total
                start(remote(ps.at[k, j], gr.at[k, back(j)], p_s.at[k, j],
                             p_r.at[k, back(j)], plane(ORD[k], j)))

    def grad_part(k, j):
        rows = pl.ds(j * TOK, TOK) if isinstance(j, int) else pl.ds(pl.multiple_of(j * TOK, TOK), TOK)
        return lax.dot_general(cot_v[k, rows, :], w_v[k], (((1,), (1,)), ((), ())),
                               preferred_element_type=F32)

    def grad_add(k, first):
        def tile(j, _):
            part = grad_part(k, j)
            hg_acc[j] = part if first else hg_acc[j] + part
            return 0

        lax.fori_loop(0, 4, tile, 0)

    def grad_sends(j):
        hg_s[j] = (hg_acc[j] + grad_part(3, j)).astype(BF16)
        if j == 0:
            copy = pltpu.make_async_copy(hg_s.at[0], hg_r.at[y], g_r.at[y])
            copy.start()
        else:
            start(remote(hg_s.at[j], hg_r.at[y], g_s.at[j], g_r.at[y], plane(0, j)))

    y_sends(0)
    w_sends()
    home()
    hidden_sends()
    pending = []
    for i in range(len(STEPS) + 2):
        if i < len(STEPS):
            k, j = STEPS[i]
            if j:
                arrived(cot_v.at[k, rows_at(j, x)], y_r.at[k, j], y_s.at[k, j])
            mine = cot_v.at[k, rows_at(j, x)]
            start(remote(mine, mine, xr_s.at[k, j], fl_r.at[k, j], right))
            start(remote(mine, mine, xl_s.at[k, j], fr_r.at[k, j], left))
            if i in (0, 4, 8):
                y_sends(k + 1)
        if 1 <= i <= len(STEPS):
            k, j = STEPS[i - 1]
            from_left = cot_v.at[k, rows_at(j, (x + 3) % 4)]
            from_right = cot_v.at[k, rows_at(j, (x + 1) % 4)]
            arrived(from_left, fl_r.at[k, j], xr_s.at[k, j])
            arrived(from_right, fr_r.at[k, j], xl_s.at[k, j])
            block, device = (from_left, right) if j in RIGHT else (from_right, left)
            start(remote(block, block, xf_s.at[k, j], xf_r.at[k, j], device))
        for k in pending:
            term_sends(k)
        pending = []
        if i >= 2:
            k, j = STEPS[i - 2]
            arrived(cot_v.at[k, rows_at(j, (x + 2) % 4)], xf_r.at[k, j], xf_s.at[k, j])
            if i == 3:
                w_near()
            if i == 5:
                hidden_arrived()
            if i == 8:
                w_far()
            if k == 3:
                if j:
                    grad_sends(j)
            elif STEPS[i - 1][0] != k:
                term(k)
                pending.append(k)
                if k == 1:
                    w_other(1)
                    grad_add(1, True)
                if k == 2:
                    w_other(2)
                    grad_add(2, False)
                    w_other(0)
                    grad_add(0, False)
                    w_other(3)
    term(3)
    grad_sends(0)
    term_sends(3)

    for yy in range(4):
        arrived(hg_r.at[yy], g_r.at[yy], g_s.at[0])

    stores = []

    def result(r, _):
        rows = pl.ds(pl.multiple_of(r * 32, 32), 32)
        p = [hg_r[q, rows, :].astype(F32) for q in range(4)]
        grad = jnp.concatenate(
            [p[0][:, :384], p[0][:, 384:] + p[1][:, :128], p[1][:, 128:],
             p[2][:, :384], p[2][:, 384:] + p[3][:, :128], p[3][:, 128:]], axis=1)
        ug_v[rows, :] = (grad * act_v[rows, :]).astype(BF16)
        gg_v[rows, :] = (grad * fac_v[rows, :]).astype(BF16)
        return 0

    for half in range(2):
        lax.fori_loop(half * 4, half * 4 + 4, result, 0)
        rows = pl.ds(half * 128, 128)
        for n, (src, dst) in enumerate(((ug_v, ug_ref), (gg_v, gg_ref))):
            stores.append(pltpu.make_async_copy(src.at[rows], dst.at[rows], out_s.at[half * 2 + n]))
            stores[-1].start()
    for j in (0, 1, 3, 2):
        total = None
        for k in range(4):
            if (k, j) != (3, 0):
                arrived(gr.at[k, j], p_r.at[k, j], p_s.at[k, j])
            part = gr[k, j].astype(F32)
            total = part if total is None else total + part
        gp_v[quarter_rows(j), :] = total * unscale
        stores.append(pltpu.make_async_copy(
            gp_v.at[quarter_rows(j)], gp_ref.at[quarter_rows(j)], out_s.at[4 + j]))
        stores[-1].start()
    for copy in sent:
        copy.wait_send()
    for store in stores:
        store.wait()


def grads(gate_pre, up_pre, cotangent, w_prev):
    def dma(*shape):
        return pltpu.SemaphoreType.DMA(shape)

    any_spec = pl.BlockSpec(memory_space=pl.ANY)
    scratch = [
        pltpu.VMEM((TOK, HID), BF16),
        pltpu.VMEM((TOK, HID), BF16),
        pltpu.VMEM((TOK, HID), F32),
        pltpu.VMEM((TOK, HID), F32),
        pltpu.VMEM((HID, TOK), BF16),
        pltpu.VMEM((QUARTER, 4 * TOK), BF16),
        pltpu.VMEM((4, 4 * TOK, CHUNK), BF16),
        pltpu.VMEM((4, WIDE, CHUNK), BF16),
        pltpu.VMEM((4, 4, QUARTER, SHARD), BF16),
        pltpu.VMEM((4, 4, QUARTER, SHARD), BF16),
        pltpu.VMEM((4, QUARTER, SHARD), F32),
        pltpu.VMEM((4, 4, QUARTER, SHARD), BF16),
        pltpu.VMEM((4, 4, QUARTER, SHARD), BF16),
        pltpu.VMEM((4, TOK, WIDE), F32),
        pltpu.VMEM((4, TOK, WIDE), BF16),
        pltpu.VMEM((4, TOK, WIDE), BF16),
        pltpu.VMEM((TOK, HID), BF16),
        pltpu.VMEM((TOK, HID), BF16),
        pltpu.VMEM((HID, SHARD), F32),
        dma(8), dma(4), dma(4), dma(4, 4), dma(4, 4),
        dma(4, 4), dma(4, 4), dma(4, 4), dma(4, 4), dma(4, 4), dma(4, 4),
        dma(4, 4), dma(4, 4), dma(4, 4), dma(4, 4),
        dma(4), dma(4), dma(4), dma(4),
        dma(4), dma(4), dma(4, 4), dma(4, 4), dma(8),
    ]
    return pl.pallas_call(
        kernel,
        out_shape=(
            jax.ShapeDtypeStruct((TOK, HID), BF16),
            jax.ShapeDtypeStruct((TOK, HID), BF16),
            jax.ShapeDtypeStruct((HID, SHARD), F32),
        ),
        in_specs=[any_spec] * 4,
        out_specs=(any_spec,) * 3,
        scratch_shapes=scratch,
        compiler_params=pltpu.CompilerParams(
            collective_id=0, has_side_effects=True, vmem_limit_bytes=52 * 2**20
        ),
        cost_estimate=pl.CostEstimate(
            flops=4 * TOK * HID * 4096, bytes_accessed=8 * 2**20, transcendentals=TOK * HID
        ),
    )(gate_pre, up_pre, cotangent, w_prev)


def body(gate_pre, up_pre, cotangent, w_prev, param_next, grad_next, moment_one, moment_two):
    gate_grad, up_grad, grad_prev = grads(gate_pre, up_pre, cotangent, w_prev)
    moment_one_f = beta_first * moment_one.astype(jnp.float32) + (1.0 - beta_first) * grad_next
    moment_two_f = (
        beta_second * moment_two.astype(jnp.float32) + (1.0 - beta_second) * grad_next * grad_next
    )
    first_fix = 1.0 - beta_first**STEP
    second_fix = 1.0 - beta_second**STEP
    adam_step = (
        moment_one_f / first_fix / (jnp.sqrt(moment_two_f / second_fix) + epsilon)
        + decay_rate * param_next
    )
    param_new = param_next - learn_rate * adam_step
    return (
        gate_grad,
        up_grad,
        grad_prev,
        param_new,
        moment_one_f.astype(jnp.bfloat16),
        moment_two_f.astype(jnp.bfloat16),
        adam_step,
    )


def solution(mesh):
    in_specs = (
        P("dp", "tensor"),
        P("dp", "tensor"),
        P(("dp", "tensor"), None),
        P("tensor", "dp"),
        P("tensor", "dp"),
        P("tensor", "dp"),
        P("tensor", "dp"),
        P("tensor", "dp"),
    )
    out_specs = (
        P("dp", "tensor"),
        P("dp", "tensor"),
        P("tensor", "dp"),
        P("tensor", "dp"),
        P("tensor", "dp"),
        P("tensor", "dp"),
        P("tensor", "dp"),
    )
    return jax.shard_map(body, mesh=mesh, in_specs=in_specs, out_specs=out_specs, check_vma=False)
```

time: 395 us -> 135 us (0.34)
  waiting for transfers between devices: 328 us -> 0 us
  Pallas kernels: 0 us -> 125 us
  matrix products: 28.2 us -> 0 us
  local copies, waits for them, and re-layouts: 20.9 us -> 5.92 us
  between operations: 13.8 us -> 0.69 us
    all_gather x2 -> x0, waiting for transfers between devices: 179 us -> none  [the longest x1 119 us: body(): weight_full = lax.all_gather(w_prev, 'dp', axis=1, tiled=True)]
    unnamed x4 -> x0, waiting for transfers between devices: 148 us -> none
    pallas_call x0 -> x1, Pallas kernels: none -> 125 us  [grads(): pl.pallas_call(kernel, out_shape=(jax.ShapeDtypeStruct((TOK, HID), BF16),...]
    dot_general x2 -> x0, matrix products: 28.2 us -> none  [the longest x1 16.6 us: body(): lax.dot_general(cotangent_all, weight_full, (((1,), (1,)), ((), ())), pre...]
    unnamed x12 -> x19, local copies, waits for them, and re-layouts: 20.9 us -> 5.92 us
  transfers between devices with their start and end apart: 3 -> 0, of which waited for: 3 -> 0; matrix products, arithmetic and copies ran while one was open for 1% -> 0% of each run, Pallas kernels for 0% -> 0%
where the time goes in v1:
time: 135 us; the launch traced here: 134 us
  Pallas kernels  125 us (93%)
  local copies, waits for them, and re-layouts  5.92 us (4%)
  other arithmetic  2.57 us (2%)
    pallas_call x1, Pallas kernels, grads(): pl.pallas_call(kernel, out_shape=(jax.ShapeDtypeStruct((TOK, HID), BF16),...  125 us
    unnamed x19, local copies, waits for them, and re-layouts  5.92 us

profile of v1, /device:TPU:1, one launch (start us, length us, event | category | flops | bytes accessed | tf_op | source)
XLA Modules:
  0.0 134.3 jit_solution(11091535979909736124)
XLA Ops:
  0.6 0.0 copy-start
  0.6 1.0 copy-done
  1.7 0.0 copy-start.1
  1.7 0.9 copy-done.1
  2.6 0.0 copy-start.4
  2.6 0.0 copy-start.5
  2.6 0.0 copy-start.6
  2.6 0.0 copy-start.7
  2.6 125.1 %shard_map.135 = (bf16[256,1792]{1,0:T(8,128)(2,1)S(1)}, bf16[256,1792]{1,0:T(8,128)(2,1)}, f32[1792,128]{1,0:T(8,128)}) custom-call(bf16[256,1792]{1,0:T(8,128)(2,1)} %gate_ref.1, bf16[256,1792]{1,0:T(8,128)(2,1)} %up_ref.1, bf16[32,4096]{1,0:T(8,128)(2,1)S(1)} %copy-done.1, bf16[1792,128]{1,0:T(8,128)(2,1)S(1)} %copy-done), custom_call_target="tpu_custom_call" | custom-call | flops 7516192768 | bytes 8388608 | tf_op jit(solution)/shard_map/pallas_call | solution.py:345
  127.8 0.0 copy-done.4
  127.8 0.0 copy-done.5
  127.8 0.0 copy-done.6
  127.8 0.0 copy-done.7
  127.8 2.6 %multiply_subtract_fusion = (f32[1792,128]{1,0:T(8,128)}, f32[1792,128]{1,0:T(8,128)}, bf16[1792,128]{1,0:T(8,128)(2,1)}, bf16[1792,128]{1,0:T(8,128)(2,1)}) fusion(f32[1792,128]{1,0:T(8,128)S(1)} %copy-done.4, f32[1792,128]{1,0:T(8,128)S(1)} %copy-done.5, bf16[1792,128]{1,0:T(8,128)(2,1)S(1)} %copy-done.6, bf16[1792,128]{1,0:T(8,128)(2,1)S(1)} %copy-done.7), kind=kLoop, calls=%fused_computation.2 | loop fusion | flops 4358144 | bytes 5505024 | tf_op jit(solution)/shard_map/sub | solution.py:376
  130.4 0.0 copy-start.3
  130.4 0.9 copy.18
  131.3 0.6 copy-done.3
  131.9 0.0 copy-start.2
  131.9 0.9 copy.19
  132.8 0.6 copy-done.2
  133.4 0.9 copy.20
Async XLA Ops:
  0.6 1.0 copy-start
  1.7 0.9 copy-start.1
  2.6 125.2 %copy-start.4 = (f32[1792,128]{1,0:T(8,128)S(1)}, f32[1792,128]{1,0:T(8,128)}, u32[]{:S(2)}) copy-start(f32[1792,128]{1,0:T(8,128)} %param.12) | copy-start | bytes 2752516
  2.6 125.2 %copy-start.5 = (f32[1792,128]{1,0:T(8,128)S(1)}, f32[1792,128]{1,0:T(8,128)}, u32[]{:S(2)}) copy-start(f32[1792,128]{1,0:T(8,128)} %param.13) | copy-start | bytes 2752516
  2.6 125.2 %copy-start.6 = (bf16[1792,128]{1,0:T(8,128)(2,1)S(1)}, bf16[1792,128]{1,0:T(8,128)(2,1)}, u32[]{:S(2)}) copy-start(bf16[1792,128]{1,0:T(8,128)(2,1)} %param.15) | copy-start | bytes 1376260
  2.6 125.2 %copy-start.7 = (bf16[1792,128]{1,0:T(8,128)(2,1)S(1)}, bf16[1792,128]{1,0:T(8,128)(2,1)}, u32[]{:S(2)}) copy-start(bf16[1792,128]{1,0:T(8,128)(2,1)} %param.14) | copy-start | bytes 1376260
  130.4 1.5 %copy-start.3 = (bf16[256,1792]{1,0:T(8,128)(2,1)S(1)}, bf16[256,1792]{1,0:T(8,128)(2,1)}, u32[]{:S(2)}) copy-start(bf16[256,1792]{1,0:T(8,128)(2,1)} %get-tuple-element.25) | copy-start | bytes 2752516
  131.9 1.5 %copy-start.2 = (f32[1792,128]{1,0:T(8,128)S(1)}, f32[1792,128]{1,0:T(8,128)}, u32[]{:S(2)}) copy-start(f32[1792,128]{1,0:T(8,128)} %get-tuple-element.26) | copy-start | bytes 2752516

commit v2 on v1

--- a/solution.py
+++ b/solution.py
@@ -21,8 +21,25 @@
 TOK, HID, QUARTER, WIDE, CHUNK, SHARD = 256, 1792, 448, 512, 1024, 128
 ORD = (2, 1, 3, 0)
 SLOT = {o: k for k, o in enumerate(ORD)}
-STEPS = [(k, j) for k in range(3) for j in (0, 1, 3, 2)] + [(3, j) for j in (2, 3, 1, 0)]
 RIGHT = (0, 3)
+ORDER = (
+    ("wsend",), ("ysend", 0), ("own", 0, 0), ("ysend", 1), ("own", 1, 0), ("farr",), ("ysend", 2),
+    ("home", 0), ("wown", 1), ("own", 2, 0), ("wown", 2), ("own", 0, 3), ("own", 0, 2),
+    ("home", 1), ("own", 1, 1), ("own", 0, 1), ("fwd", 0, 2), ("fwd", 0, 0), ("wown", 3),
+    ("own", 1, 2), ("wnear", 2), ("home", 2), ("own", 1, 3), ("home", 3), ("fwd", 0, 3),
+    ("hsend",), ("wnear", 1), ("fwd", 0, 1), ("wown", 0), ("done", 0, 0), ("fwd", 1, 2),
+    ("done", 0, 2), ("wnear", 3), ("own", 2, 1), ("harr",), ("fwd", 1, 3), ("own", 2, 3),
+    ("fwd", 1, 1), ("done", 0, 3), ("done", 0, 1), ("ysend", 3), ("fwd", 1, 0), ("wnear", 0),
+    ("term", 0), ("own", 2, 2), ("tsend", 0), ("fwd", 2, 1), ("done", 1, 3), ("done", 1, 1),
+    ("done", 1, 0), ("woth", 2), ("done", 1, 2), ("wfar",), ("fwd", 2, 3), ("term", 1),
+    ("fwd", 2, 2), ("fwd", 2, 0), ("own", 3, 0), ("own", 3, 2), ("woth", 0), ("woth", 1),
+    ("gadd", 0), ("own", 3, 3), ("tsend", 1), ("done", 2, 1), ("done", 2, 0), ("done", 2, 3),
+    ("done", 2, 2), ("term", 2), ("gadd", 1), ("tsend", 2), ("fwd", 3, 0), ("fwd", 3, 2),
+    ("own", 3, 1), ("done", 3, 2), ("fwd", 3, 3), ("gadd", 2), ("woth", 3), ("fwd", 3, 1),
+    ("gsend", 2), ("done", 3, 0), ("done", 3, 3), ("gsend", 3), ("done", 3, 1), ("ladd", 3),
+    ("gsend", 1), ("ladd", 2), ("ladd", 1), ("gsend", 0), ("lterms",), ("lsends",), ("gres",),
+    ("pres",),
+)
 
 
 def back(j):
@@ -31,10 +48,10 @@
 
 def kernel(
     gate_ref, up_ref, cot_ref, w_ref, gg_ref, ug_ref, gp_ref,
-    gate_v, up_v, act_v, fac_v, hidh, hidt, cot_v, w_v, px_s, px_r, pown, ps, gr,
+    gate_v, up_v, act_v, fac_v, hidh, hidt, cot_v, w_v, px_s, px_r, pown, pacc, ps, pq, pz, py,
     hg_acc, hg_s, hg_r, gg_v, ug_v, gp_v,
     ld, zl_s, zl_r, y_s, y_r, xr_s, xl_s, fl_r, fr_r, xf_s, xf_r, w_s, w_r, wc_s, wc_r,
-    h_s, h_r, g_s, g_r, pc_s, pc_r, p_s, p_r, out_s,
+    h_s, h_r, g_s, g_r, pc_s, pc_r, q_s, q_r, p_s, p_r, py_s, py_r, l_s, l_r, out_s, ready,
 ):
     dp, tn = lax.axis_index("dp"), lax.axis_index("tensor")
     c, y, zh = dp % 2, (dp // 2) % 4, dp // 8
@@ -55,6 +72,7 @@
         )
 
     sent = []
+    done_once = set()
 
     def start(copy):
         copy.start()
@@ -69,11 +87,36 @@
     def rows_at(j, xx, n=64, extra=0):
         return pl.ds(pl.multiple_of(j * TOK + xx * 64 + extra, 32), n)
 
-    peers = [plane(o, j) for o in range(4) for j in range(4) if (o, j) != (0, 0)]
-    peers += [other_core, other_zl, right, left]
+    near = [plane(0, j)[0] for j in (1, 2, 3)]
+    near = [(d - c, tn) for d in near] + [(dp - c, d[1]) for d in (other_zl, right, left)]
+    far = [(plane(o, 0)[0] - c + 1, tn) for o in (1, 3)]
     barrier = pltpu.get_barrier_semaphore()
-    for peer in peers:
+    for peer in near + far:
         pl.semaphore_signal(barrier, inc=1, device_id=peer, device_id_type=MESH)
+
+    @pl.when(c == 1)
+    def _():
+        pl.semaphore_signal(barrier, inc=1, device_id=other_core, device_id_type=MESH)
+
+    def near_ready():
+        @pl.when(c == 0)
+        def _():
+            pl.semaphore_wait(barrier, 2 * len(near) + 1)
+            pl.semaphore_signal(ready, inc=1, device_id=other_core, device_id_type=MESH)
+
+        @pl.when(c == 1)
+        def _():
+            pl.semaphore_wait(ready, 1)
+
+    def far_ready():
+        @pl.when(c == 1)
+        def _():
+            pl.semaphore_wait(barrier, 2 * len(far))
+            pl.semaphore_signal(ready, inc=1, device_id=other_core, device_id_type=MESH)
+
+        @pl.when(c == 0)
+        def _():
+            pl.semaphore_wait(ready, 1)
 
     own_rows = rows_at(0, x, 32, zl * 32)
     loads = []
@@ -99,7 +142,7 @@
     pad = pl.ds(pl.multiple_of((1 - y % 2) * QUARTER, 64), 64)
     for k in range(4):
         w_v[k, pad, :] = jnp.zeros((64, CHUNK), BF16)
-    pl.semaphore_wait(barrier, len(peers))
+    near_ready()
 
     for k in range(4):
         start(remote(cot_ref.at[:, chunk_cols(k)], cot_v.at[k, own_rows],
@@ -114,11 +157,9 @@
                          y_s.at[k, j], y_r.at[k, back(j)], plane(0, j)))
 
     def w_sends():
-        for o, j in [(1, 0), (3, 0), (1, 1), (3, 1), (1, 3), (3, 3), (1, 2), (3, 2),
-                     (0, 1), (0, 3), (0, 2)]:
-            k = SLOT[back(o)]
-            start(remote(w_ref.at[quarter_rows(j)], w_v.at[k, w_rows(j), w_cols(0, c)],
-                         w_s.at[k, back(j)], w_r.at[k, back(j)], plane(o, j)))
+        for j in (1, 3, 2):
+            start(remote(w_ref.at[quarter_rows(j)], w_v.at[3, w_rows(j), w_cols(0, c)],
+                         w_s.at[3, back(j)], w_r.at[3, back(j)], plane(0, j)))
 
     def w_block(k, j, cc):
         return w_v.at[k, w_rows(0), w_cols(j, cc)]
@@ -130,27 +171,35 @@
             arrived(w_block(k, j, c), w_r.at[k, j], w_s.at[k, j])
         start(remote(w_block(k, j, c), w_block(k, j, c), wc_s.at[k, j], wc_r.at[k, j], other_core))
 
-    def w_near():
-        for k, o, blocks in ((SLOT[1], 3, (0, 1)), (SLOT[3], 1, (2, 3))):
-            for j in range(4):
-                w_arrived(k, j)
-                if j in blocks:
-                    start(remote(w_block(k, j, c), w_block(0, j, c),
-                                 w_s.at[0, j], w_r.at[0, j], plane(o, 0)))
-        for j in range(4):
-            w_arrived(3, j)
+    def w_own(j):
+        w_arrived(3, j)
+        for o in (1, 3):
+            k = SLOT[back(o)]
+            start(remote(w_block(3, j, c), w_block(k, j, c), w_s.at[k, j], w_r.at[k, j],
+                         plane(o, 0)))
+
+    def w_near(j):
+        for o, passed in ((3, (0, 1)), (1, (2, 3))):
+            k = SLOT[back(o)]
+            w_arrived(k, j)
+            if j in passed:
+                start(remote(w_block(k, j, c), w_block(SLOT[2], j, c),
+                             w_s.at[SLOT[2], j], w_r.at[SLOT[2], j], plane(o, 0)))
 
     def w_far():
         for j in range(4):
-            w_arrived(0, j)
+            w_arrived(SLOT[2], j)
 
     def w_other(k):
         for j in range(4):
             arrived(w_block(k, j, 1 - c), wc_r.at[k, j], wc_s.at[k, j])
 
-    def home():
-        loads[4].wait()
-        loads[5].wait()
+    HOME = (0, 4, 8, 11, 14)
+
+    def home(part):
+        if part == 0:
+            loads[4].wait()
+            loads[5].wait()
 
         def block(f, _):
             cols = pl.ds(pl.multiple_of(f * 128, 128), 128)
@@ -163,7 +212,7 @@
             hidh[cols, :] = (act * u).T.astype(BF16)
             return 0
 
-        lax.fori_loop(0, HID // 128, block, 0)
+        lax.fori_loop(HOME[part], HOME[part + 1], block, 0)
 
     def hidden_sends():
         for j in (2, 1, 3):
@@ -189,21 +238,67 @@
 
     def term_sends(k):
         arrived(px_r.at[k], pc_r.at[k], pc_s.at[k])
+        if k:
+            passed = (0, 1) if k == 1 else (2, 3)
+            part = pl.ds(passed[0], 2)
+            arrived(pq.at[part], q_r.at[k - 1], q_s.at[k - 1])
+        for j in range(4):
+            total = pown[j] + px_r[k, j].astype(F32)
+            if k and j in passed:
+                total = total + pq[j].astype(F32)
+            ps[k, j] = total.astype(BF16)
+        if k == 0:
+            for n, o in enumerate((1, 3)):
+                part = pl.ds(2 * n, 2)
+                start(remote(ps.at[0, part], pq.at[part], q_s.at[n], q_r.at[n], plane(o, 0)))
+        else:
+            start(remote(ps.at[k], pz.at[k - 1], p_s.at[k], p_r.at[k], plane(ORD[k], 0)))
+
+    def last_part(block, j):
+        cols = pl.ds(pl.multiple_of(((y + j) % 4) * 256, 256), 256)
+        return jnp.dot(hidt[:, pl.ds(block * TOK, TOK)], cot_v[3, pl.ds(block * TOK, TOK), cols],
+                       preferred_element_type=F32)
+
+    def last_add(block):
+        first = ("ladd",) not in done_once
+        done_once.add(("ladd",))
+
+        def tile(j, _):
+            part = last_part(block, j)
+            pacc[j] = part if first else pacc[j] + part
+            return 0
+
+        lax.fori_loop(0, 4, tile, 0)
+
+    def last_terms():
         for j in (2, 1, 3, 0):
-            total = (pown[j] + px_r[k, j].astype(F32)).astype(BF16)
-            if (k, j) == (3, 0):
-                gr[3, 0] = total
+            part = pacc[j] + last_part(0, j)
+            low, high = part[:, :SHARD], part[:, SHARD:]
+            px_s[3, j] = jnp.where(c == 0, high, low).astype(BF16)
+            start(remote(px_s.at[3, j], px_r.at[3, j], l_s.at[j], l_r.at[j], other_core))
+            pown[j] = jnp.where(c == 0, low, high)
+
+    def last_sends():
+        for k in (1, 2):
+            arrived(pz.at[k - 1], p_r.at[k], p_s.at[k])
+        for j in (2, 1, 3, 0):
+            arrived(px_r.at[3, j], l_r.at[j], l_s.at[j])
+            total = pown[j] + px_r[3, j].astype(F32) + (pz[0, j].astype(F32) + pz[1, j].astype(F32))
+            if j:
+                ps[3, j] = total.astype(BF16)
+                start(remote(ps.at[3, j], py.at[back(j)], py_s.at[j], py_r.at[back(j)], plane(0, j)))
             else:
-                ps[k, j] = total
-                start(remote(ps.at[k, j], gr.at[k, back(j)], p_s.at[k, j],
-                             p_r.at[k, back(j)], plane(ORD[k], j)))
+                gp_v[quarter_rows(0), :] = total * unscale
 
     def grad_part(k, j):
         rows = pl.ds(j * TOK, TOK) if isinstance(j, int) else pl.ds(pl.multiple_of(j * TOK, TOK), TOK)
         return lax.dot_general(cot_v[k, rows, :], w_v[k], (((1,), (1,)), ((), ())),
                                preferred_element_type=F32)
 
-    def grad_add(k, first):
+    def grad_add(k):
+        first = ("gadd",) not in done_once
+        done_once.add(("gadd",))
+
         def tile(j, _):
             part = grad_part(k, j)
             hg_acc[j] = part if first else hg_acc[j] + part
@@ -219,62 +314,23 @@
         else:
             start(remote(hg_s.at[j], hg_r.at[y], g_s.at[j], g_r.at[y], plane(0, j)))
 
-    y_sends(0)
-    w_sends()
-    home()
-    hidden_sends()
-    pending = []
-    for i in range(len(STEPS) + 2):
-        if i < len(STEPS):
-            k, j = STEPS[i]
-            if j:
-                arrived(cot_v.at[k, rows_at(j, x)], y_r.at[k, j], y_s.at[k, j])
-            mine = cot_v.at[k, rows_at(j, x)]
-            start(remote(mine, mine, xr_s.at[k, j], fl_r.at[k, j], right))
-            start(remote(mine, mine, xl_s.at[k, j], fr_r.at[k, j], left))
-            if i in (0, 4, 8):
-                y_sends(k + 1)
-        if 1 <= i <= len(STEPS):
-            k, j = STEPS[i - 1]
-            from_left = cot_v.at[k, rows_at(j, (x + 3) % 4)]
-            from_right = cot_v.at[k, rows_at(j, (x + 1) % 4)]
-            arrived(from_left, fl_r.at[k, j], xr_s.at[k, j])
-            arrived(from_right, fr_r.at[k, j], xl_s.at[k, j])
-            block, device = (from_left, right) if j in RIGHT else (from_right, left)
-            start(remote(block, block, xf_s.at[k, j], xf_r.at[k, j], device))
-        for k in pending:
-            term_sends(k)
-        pending = []
-        if i >= 2:
-            k, j = STEPS[i - 2]
-            arrived(cot_v.at[k, rows_at(j, (x + 2) % 4)], xf_r.at[k, j], xf_s.at[k, j])
-            if i == 3:
-                w_near()
-            if i == 5:
-                hidden_arrived()
-            if i == 8:
-                w_far()
-            if k == 3:
-                if j:
-                    grad_sends(j)
-            elif STEPS[i - 1][0] != k:
-                term(k)
-                pending.append(k)
-                if k == 1:
-                    w_other(1)
-                    grad_add(1, True)
-                if k == 2:
-                    w_other(2)
-                    grad_add(2, False)
-                    w_other(0)
-                    grad_add(0, False)
-                    w_other(3)
-    term(3)
-    grad_sends(0)
-    term_sends(3)
-
-    for yy in range(4):
-        arrived(hg_r.at[yy], g_r.at[yy], g_s.at[0])
+    def own(k, j):
+        if j:
+            arrived(cot_v.at[k, rows_at(j, x)], y_r.at[k, j], y_s.at[k, j])
+        mine = cot_v.at[k, rows_at(j, x)]
+        start(remote(mine, mine, xr_s.at[k, j], fl_r.at[k, j], right))
+        start(remote(mine, mine, xl_s.at[k, j], fr_r.at[k, j], left))
+
+    def forward(k, j):
+        from_left = cot_v.at[k, rows_at(j, (x + 3) % 4)]
+        from_right = cot_v.at[k, rows_at(j, (x + 1) % 4)]
+        arrived(from_left, fl_r.at[k, j], xr_s.at[k, j])
+        arrived(from_right, fr_r.at[k, j], xl_s.at[k, j])
+        block, device = (from_left, right) if j in RIGHT else (from_right, left)
+        start(remote(block, block, xf_s.at[k, j], xf_r.at[k, j], device))
+
+    def done(k, j):
+        arrived(cot_v.at[k, rows_at(j, (x + 2) % 4)], xf_r.at[k, j], xf_s.at[k, j])
 
     stores = []
 
@@ -288,23 +344,35 @@
         gg_v[rows, :] = (grad * fac_v[rows, :]).astype(BF16)
         return 0
 
-    for half in range(2):
-        lax.fori_loop(half * 4, half * 4 + 4, result, 0)
-        rows = pl.ds(half * 128, 128)
-        for n, (src, dst) in enumerate(((ug_v, ug_ref), (gg_v, gg_ref))):
-            stores.append(pltpu.make_async_copy(src.at[rows], dst.at[rows], out_s.at[half * 2 + n]))
+    def grad_results():
+        for yy in range(4):
+            arrived(hg_r.at[yy], g_r.at[yy], g_s.at[0])
+        for half in range(2):
+            lax.fori_loop(half * 4, half * 4 + 4, result, 0)
+            rows = pl.ds(half * 128, 128)
+            for n, (src, dst) in enumerate(((ug_v, ug_ref), (gg_v, gg_ref))):
+                stores.append(pltpu.make_async_copy(
+                    src.at[rows], dst.at[rows], out_s.at[half * 2 + n]))
+                stores[-1].start()
+
+    def term_results():
+        for j in (0, 1, 3, 2):
+            if j:
+                arrived(py.at[j], py_r.at[j], py_s.at[j])
+                gp_v[quarter_rows(j), :] = py[j].astype(F32) * unscale
+            stores.append(pltpu.make_async_copy(
+                gp_v.at[quarter_rows(j)], gp_ref.at[quarter_rows(j)], out_s.at[4 + j]))
             stores[-1].start()
-    for j in (0, 1, 3, 2):
-        total = None
-        for k in range(4):
-            if (k, j) != (3, 0):
-                arrived(gr.at[k, j], p_r.at[k, j], p_s.at[k, j])
-            part = gr[k, j].astype(F32)
-            total = part if total is None else total + part
-        gp_v[quarter_rows(j), :] = total * unscale
-        stores.append(pltpu.make_async_copy(
-            gp_v.at[quarter_rows(j)], gp_ref.at[quarter_rows(j)], out_s.at[4 + j]))
-        stores[-1].start()
+
+    steps = dict(
+        ysend=y_sends, own=own, fwd=forward, done=done, wsend=w_sends, farr=far_ready, wown=w_own,
+        wnear=w_near, wfar=w_far, woth=w_other, home=home, hsend=hidden_sends,
+        harr=hidden_arrived, term=term, tsend=term_sends, gadd=grad_add, ladd=last_add,
+        gsend=grad_sends, lterms=last_terms, lsends=last_sends, gres=grad_results,
+        pres=term_results,
+    )
+    for name, *place in ORDER:
+        steps[name](*place)
     for copy in sent:
         copy.wait_send()
     for store in stores:
@@ -328,8 +396,11 @@
         pltpu.VMEM((4, 4, QUARTER, SHARD), BF16),
         pltpu.VMEM((4, 4, QUARTER, SHARD), BF16),
         pltpu.VMEM((4, QUARTER, SHARD), F32),
+        pltpu.VMEM((4, QUARTER, 256), F32),
         pltpu.VMEM((4, 4, QUARTER, SHARD), BF16),
-        pltpu.VMEM((4, 4, QUARTER, SHARD), BF16),
+        pltpu.VMEM((4, QUARTER, SHARD), BF16),
+        pltpu.VMEM((2, 4, QUARTER, SHARD), BF16),
+        pltpu.VMEM((4, QUARTER, SHARD), BF16),
         pltpu.VMEM((4, TOK, WIDE), F32),
         pltpu.VMEM((4, TOK, WIDE), BF16),
         pltpu.VMEM((4, TOK, WIDE), BF16),
@@ -340,7 +411,9 @@
         dma(4, 4), dma(4, 4), dma(4, 4), dma(4, 4), dma(4, 4), dma(4, 4),
         dma(4, 4), dma(4, 4), dma(4, 4), dma(4, 4),
         dma(4), dma(4), dma(4), dma(4),
-        dma(4), dma(4), dma(4, 4), dma(4, 4), dma(8),
+        dma(4), dma(4), dma(2), dma(2), dma(4), dma(4), dma(4), dma(4),
+        dma(4), dma(4), dma(8),
+        pltpu.SemaphoreType.REGULAR,
     ]
     return pl.pallas_call(
         kernel,
@@ -353,7 +426,7 @@
         out_specs=(any_spec,) * 3,
         scratch_shapes=scratch,
         compiler_params=pltpu.CompilerParams(
-            collective_id=0, has_side_effects=True, vmem_limit_bytes=52 * 2**20
+            collective_id=0, has_side_effects=True, vmem_limit_bytes=62 * 2**20
         ),
         cost_estimate=pl.CostEstimate(
             flops=4 * TOK * HID * 4096, bytes_accessed=8 * 2**20, transcendentals=TOK * HID

time: 135 us -> 110 us (0.81)
  Pallas kernels: 125 us -> 102 us
  local copies, waits for them, and re-layouts: 5.92 us -> 3.95 us
    pallas_call x1, Pallas kernels: 125 us -> 102 us  [grads(): pl.pallas_call(kernel, out_shape=(jax.ShapeDtypeStruct((TOK, HID), BF16),...]
    unnamed x19 -> x13, local copies, waits for them, and re-layouts: 5.92 us -> 3.95 us
where the time goes in v2:
time: 110 us
  Pallas kernels  102 us (93%)
  local copies, waits for them, and re-layouts  3.95 us (4%)
  other arithmetic  3.81 us (3%)
    pallas_call x1, Pallas kernels, grads(): pl.pallas_call(kernel, out_shape=(jax.ShapeDtypeStruct((TOK, HID), BF16),...  102 us
    unnamed x13, local copies, waits for them, and re-layouts  3.95 us
    sub x1, other arithmetic, body(): param_new = param_next - learn_rate * adam_step  3.81 us

profile of v2, /device:TPU:1, one launch (start us, length us, event | category | flops | bytes accessed | tf_op | source)
XLA Modules:
  0.0 110.1 jit_solution(1842496918692335160)
XLA Ops:
  0.6 0.0 copy-start.3
  0.6 0.0 copy-start.4
  0.7 101.6 %shard_map.135 = (bf16[256,1792]{1,0:T(8,128)(2,1)}, bf16[256,1792]{1,0:T(8,128)(2,1)}, f32[1792,128]{1,0:T(8,128)}) custom-call(bf16[256,1792]{1,0:T(8,128)(2,1)} %gate_ref.1, bf16[256,1792]{1,0:T(8,128)(2,1)} %up_ref.1, bf16[32,4096]{1,0:T(8,128)(2,1)} %cot_ref.1, bf16[1792,128]{1,0:T(8,128)(2,1)} %w_ref.1), custom_call_target="tpu_custom_call" | custom-call | flops 7516192768 | bytes 8388608 | tf_op jit(solution)/shard_map/pallas_call | solution.py:418
  102.3 0.0 copy-done.3
  102.3 0.0 copy-done.4
  102.3 0.0 copy-start.2
  102.3 3.8 %multiply_subtract_fusion = (f32[1792,128]{1,0:T(8,128)}, f32[1792,128]{1,0:T(8,128)}, bf16[1792,128]{1,0:T(8,128)(2,1)}, bf16[1792,128]{1,0:T(8,128)(2,1)}) fusion(f32[1792,128]{1,0:T(8,128)S(1)} %copy-done.3, f32[1792,128]{1,0:T(8,128)S(1)} %copy-done.4, bf16[1792,128]{1,0:T(8,128)(2,1)} %param.15, bf16[1792,128]{1,0:T(8,128)(2,1)} %param.14), kind=kLoop, calls=%fused_computation.2 | loop fusion | flops 4358144 | bytes 5505024 | tf_op jit(solution)/shard_map/sub | solution.py:449
  106.1 0.0 copy-done.2
  106.2 0.0 copy-start.1
  106.2 0.9 copy.18
  107.1 0.6 copy-done.1
  107.7 0.0 copy-start
  107.7 0.9 copy.19
  108.6 0.6 copy-done
  109.2 0.9 copy.20
Async XLA Ops:
  0.6 101.7 %copy-start.3 = (f32[1792,128]{1,0:T(8,128)S(1)}, f32[1792,128]{1,0:T(8,128)}, u32[]{:S(2)}) copy-start(f32[1792,128]{1,0:T(8,128)} %param.12) | copy-start | bytes 2752516
  0.6 101.7 %copy-start.4 = (f32[1792,128]{1,0:T(8,128)S(1)}, f32[1792,128]{1,0:T(8,128)}, u32[]{:S(2)}) copy-start(f32[1792,128]{1,0:T(8,128)} %param.13) | copy-start | bytes 2752516
  102.3 3.8 %copy-start.2 = (bf16[256,1792]{1,0:T(8,128)(2,1)S(1)}, bf16[256,1792]{1,0:T(8,128)(2,1)}, u32[]{:S(2)}) copy-start(bf16[256,1792]{1,0:T(8,128)(2,1)} %get-tuple-element.24) | copy-start | bytes 2752516
  106.2 1.5 %copy-start.1 = (bf16[256,1792]{1,0:T(8,128)(2,1)S(1)}, bf16[256,1792]{1,0:T(8,128)(2,1)}, u32[]{:S(2)}) copy-start(bf16[256,1792]{1,0:T(8,128)(2,1)} %get-tuple-element.25) | copy-start | bytes 2752516
  107.7 1.5 %copy-start = (f32[1792,128]{1,0:T(8,128)S(1)}, f32[1792,128]{1,0:T(8,128)}, u32[]{:S(2)}) copy-start(f32[1792,128]{1,0:T(8,128)} %get-tuple-element.26) | copy-start | bytes 2752516

commit v3 on v2

--- a/solution.py
+++ b/solution.py
@@ -22,23 +22,22 @@
 ORD = (2, 1, 3, 0)
 SLOT = {o: k for k, o in enumerate(ORD)}
 RIGHT = (0, 3)
+ALONG_X = 2
 ORDER = (
-    ("wsend",), ("ysend", 0), ("own", 0, 0), ("ysend", 1), ("own", 1, 0), ("farr",), ("ysend", 2),
-    ("home", 0), ("wown", 1), ("own", 2, 0), ("wown", 2), ("own", 0, 3), ("own", 0, 2),
-    ("home", 1), ("own", 1, 1), ("own", 0, 1), ("fwd", 0, 2), ("fwd", 0, 0), ("wown", 3),
-    ("own", 1, 2), ("wnear", 2), ("home", 2), ("own", 1, 3), ("home", 3), ("fwd", 0, 3),
-    ("hsend",), ("wnear", 1), ("fwd", 0, 1), ("wown", 0), ("done", 0, 0), ("fwd", 1, 2),
-    ("done", 0, 2), ("wnear", 3), ("own", 2, 1), ("harr",), ("fwd", 1, 3), ("own", 2, 3),
-    ("fwd", 1, 1), ("done", 0, 3), ("done", 0, 1), ("ysend", 3), ("fwd", 1, 0), ("wnear", 0),
-    ("term", 0), ("own", 2, 2), ("tsend", 0), ("fwd", 2, 1), ("done", 1, 3), ("done", 1, 1),
-    ("done", 1, 0), ("woth", 2), ("done", 1, 2), ("wfar",), ("fwd", 2, 3), ("term", 1),
-    ("fwd", 2, 2), ("fwd", 2, 0), ("own", 3, 0), ("own", 3, 2), ("woth", 0), ("woth", 1),
-    ("gadd", 0), ("own", 3, 3), ("tsend", 1), ("done", 2, 1), ("done", 2, 0), ("done", 2, 3),
-    ("done", 2, 2), ("term", 2), ("gadd", 1), ("tsend", 2), ("fwd", 3, 0), ("fwd", 3, 2),
-    ("own", 3, 1), ("done", 3, 2), ("fwd", 3, 3), ("gadd", 2), ("woth", 3), ("fwd", 3, 1),
-    ("gsend", 2), ("done", 3, 0), ("done", 3, 3), ("gsend", 3), ("done", 3, 1), ("ladd", 3),
-    ("gsend", 1), ("ladd", 2), ("ladd", 1), ("gsend", 0), ("lterms",), ("lsends",), ("gres",),
-    ("pres",),
+    ("wsend",), ("ysend", 0), ("own", 0, 0), ("home", 0), ("home", 1), ("home", 2), ("home", 3),
+    ("hsend",), ("farr",), ("bown",), ("wown", 0), ("wown", 2), ("own", 0, 3), ("wown", 3),
+    ("ysend", 1), ("own", 0, 1), ("own", 0, 2), ("fwd", 0, 0), ("fwd", 0, 3), ("wown", 1),
+    ("fwd", 0, 1), ("fwd", 0, 2), ("bfwd",), ("ysend", 3), ("own", 1, 3), ("wnear", 0),
+    ("own", 1, 0), ("done", 0, 2), ("done", 0, 3), ("by", 1), ("done", 0, 0), ("wnear", 2),
+    ("harr",), ("own", 1, 1), ("done", 0, 1), ("term", 0), ("tsend", 0), ("by", 2), ("own", 1, 2),
+    ("fwd", 1, 3), ("wnear", 1), ("fwd", 1, 0), ("fwd", 1, 1), ("fwd", 1, 2), ("done", 1, 3),
+    ("by", 0), ("woth", 3), ("own", 3, 3), ("wnear", 3), ("woth", 2), ("done", 1, 2), ("woth", 1),
+    ("own", 3, 2), ("done", 1, 0), ("done", 1, 1), ("term", 1), ("own", 3, 0), ("own", 3, 1),
+    ("by", 3), ("tsend", 1), ("fwd", 3, 2), ("gadd", 1), ("fwd", 3, 3), ("wfar",), ("bdone",),
+    ("term", 2), ("done", 3, 3), ("ladd", 3), ("fwd", 3, 0), ("fwd", 3, 1), ("woth", 0),
+    ("gadd", 2), ("done", 3, 2), ("tsend", 2), ("gadd", 0), ("gsend", 2), ("gsend", 3),
+    ("ladd", 2), ("done", 3, 0), ("done", 3, 1), ("ladd", 1), ("gsend", 1), ("lterms",),
+    ("lsends",), ("gsend", 0), ("gres",), ("pres",),
 )
 
 
@@ -51,7 +50,7 @@
     gate_v, up_v, act_v, fac_v, hidh, hidt, cot_v, w_v, px_s, px_r, pown, pacc, ps, pq, pz, py,
     hg_acc, hg_s, hg_r, gg_v, ug_v, gp_v,
     ld, zl_s, zl_r, y_s, y_r, xr_s, xl_s, fl_r, fr_r, xf_s, xf_r, w_s, w_r, wc_s, wc_r,
-    h_s, h_r, g_s, g_r, pc_s, pc_r, q_s, q_r, p_s, p_r, py_s, py_r, l_s, l_r, out_s, ready,
+    h_s, h_r, g_s, g_r, pc_s, pc_r, q_s, q_r, p_s, p_r, py_s, py_r, l_s, l_r, by_s, by_r, out_s, ready,
 ):
     dp, tn = lax.axis_index("dp"), lax.axis_index("tensor")
     c, y, zh = dp % 2, (dp // 2) % 4, dp // 8
@@ -81,8 +80,8 @@
     def arrived(ref, recv, send):
         remote(ref, ref, send, recv, other_core).wait_recv()
 
-    def chunk_cols(k):
-        return pl.ds(pl.multiple_of(((zh + ORD[k]) % 4) * CHUNK, CHUNK), CHUNK)
+    def features(o, first, n):
+        return pl.ds(pl.multiple_of(((zh + o) % 4) * CHUNK + first, 512), n)
 
     def rows_at(j, xx, n=64, extra=0):
         return pl.ds(pl.multiple_of(j * TOK + xx * 64 + extra, 32), n)
@@ -121,8 +120,16 @@
     own_rows = rows_at(0, x, 32, zl * 32)
     loads = []
     for k in range(4):
-        loads.append(pltpu.make_async_copy(
-            cot_ref.at[:, chunk_cols(k)], cot_v.at[k, own_rows], ld.at[k]))
+        if k in (1, 2):
+            parts = [(o, (k - 1) * 512, 512, to) for o, to in ((1, 0), (3, 512))]
+        else:
+            parts = [(ORD[k], 0, CHUNK, 0)]
+        for o, first, n, to in parts:
+            sem = ld.at[k] if to == 0 else ld.at[6 + k]
+            loads.append(pltpu.make_async_copy(
+                cot_ref.at[:, features(o, first, n)], cot_v.at[k, own_rows, pl.ds(to, n)], sem))
+    cot_loads = ((0,), (1, 2), (3, 4), (5,))
+    gate_load, up_load, w_load = 6, 7, 8
     loads.append(pltpu.make_async_copy(gate_ref, gate_v, ld.at[4]))
     loads.append(pltpu.make_async_copy(up_ref, up_v, ld.at[5]))
 
@@ -145,12 +152,13 @@
     near_ready()
 
     for k in range(4):
-        start(remote(cot_ref.at[:, chunk_cols(k)], cot_v.at[k, own_rows],
-                     zl_s.at[k], zl_r.at[k], other_zl))
+        for n in cot_loads[k]:
+            loads[n].wait()
+        mine = cot_v.at[k, own_rows]
+        start(remote(mine, mine, zl_s.at[k], zl_r.at[k], other_zl))
     partner_rows = rows_at(0, x, 32, (1 - zl) * 32)
 
     def y_sends(k):
-        loads[k].wait()
         arrived(cot_v.at[k, partner_rows], zl_r.at[k], zl_s.at[k])
         for j in ((2, 3, 1) if k == 3 else (1, 3, 2)):
             start(remote(cot_v.at[k, rows_at(0, x)], cot_v.at[k, rows_at(back(j), x)],
@@ -162,11 +170,15 @@
                          w_s.at[3, back(j)], w_r.at[3, back(j)], plane(0, j)))
 
     def w_block(k, j, cc):
+        if k in (1, 2):
+            yy = (y + j) % 4
+            col = (k - 1) * 512 + (yy % 2) * 256 + cc * SHARD
+            return w_v.at[1 + yy // 2, w_rows(0), pl.ds(pl.multiple_of(col, SHARD), SHARD)]
         return w_v.at[k, w_rows(0), w_cols(j, cc)]
 
     def w_arrived(k, j):
         if (k, j) == (3, 0):
-            loads[6].wait()
+            loads[w_load].wait()
         else:
             arrived(w_block(k, j, c), w_r.at[k, j], w_s.at[k, j])
         start(remote(w_block(k, j, c), w_block(k, j, c), wc_s.at[k, j], wc_r.at[k, j], other_core))
@@ -198,8 +210,8 @@
 
     def home(part):
         if part == 0:
-            loads[4].wait()
-            loads[5].wait()
+            loads[gate_load].wait()
+            loads[up_load].wait()
 
         def block(f, _):
             cols = pl.ds(pl.multiple_of(f * 128, 128), 128)
@@ -226,7 +238,7 @@
 
     def term(k):
         def tile(j, _):
-            cols = pl.ds(pl.multiple_of(((y + j) % 4) * 256, 256), 256)
+            cols = pl.ds(pl.multiple_of(j * 256, 256), 256)
             part = jnp.dot(hidt[...], cot_v[k, :, cols], preferred_element_type=F32)
             low, high = part[:, :SHARD], part[:, SHARD:]
             pown[j] = jnp.where(c == 0, low, high)
@@ -239,20 +251,20 @@
     def term_sends(k):
         arrived(px_r.at[k], pc_r.at[k], pc_s.at[k])
         if k:
-            passed = (0, 1) if k == 1 else (2, 3)
-            part = pl.ds(passed[0], 2)
+            part = pl.ds(2 * (k - 1), 2)
             arrived(pq.at[part], q_r.at[k - 1], q_s.at[k - 1])
-        for j in range(4):
-            total = pown[j] + px_r[k, j].astype(F32)
-            if k and j in passed:
-                total = total + pq[j].astype(F32)
-            ps[k, j] = total.astype(BF16)
-        if k == 0:
-            for n, o in enumerate((1, 3)):
-                part = pl.ds(2 * n, 2)
+        for t in range(4):
+            total = pown[t] + px_r[k, t].astype(F32)
+            if k and t // 2 == k - 1:
+                total = total + pq[t].astype(F32)
+            ps[k, t] = total.astype(BF16)
+        for n, o in enumerate((1, 3)):
+            part = pl.ds(2 * n, 2)
+            if k == 0:
                 start(remote(ps.at[0, part], pq.at[part], q_s.at[n], q_r.at[n], plane(o, 0)))
-        else:
-            start(remote(ps.at[k], pz.at[k - 1], p_s.at[k], p_r.at[k], plane(ORD[k], 0)))
+            else:
+                start(remote(ps.at[k, part], pz.at[n, pl.ds(2 * (k - 1), 2)],
+                             p_s.at[k, n], p_r.at[k, n], plane(o, 0)))
 
     def last_part(block, j):
         cols = pl.ds(pl.multiple_of(((y + j) % 4) * 256, 256), 256)
@@ -280,10 +292,12 @@
 
     def last_sends():
         for k in (1, 2):
-            arrived(pz.at[k - 1], p_r.at[k], p_s.at[k])
+            for n in range(2):
+                arrived(pz.at[n, pl.ds(2 * (k - 1), 2)], p_r.at[k, n], p_s.at[k, n])
         for j in (2, 1, 3, 0):
             arrived(px_r.at[3, j], l_r.at[j], l_s.at[j])
-            total = pown[j] + px_r[3, j].astype(F32) + (pz[0, j].astype(F32) + pz[1, j].astype(F32))
+            yy = (y + j) % 4
+            total = pown[j] + px_r[3, j].astype(F32) + (pz[0, yy].astype(F32) + pz[1, yy].astype(F32))
             if j:
                 ps[3, j] = total.astype(BF16)
                 start(remote(ps.at[3, j], py.at[back(j)], py_s.at[j], py_r.at[back(j)], plane(0, j)))
@@ -364,7 +378,40 @@
                 gp_v.at[quarter_rows(j)], gp_ref.at[quarter_rows(j)], out_s.at[4 + j]))
             stores[-1].start()
 
+    def b_rows(j, n, first=0, size=64):
+        return rows_at(j, (x + (0, 3, 1, 2)[n]) % 4, size, first)
+
+    def b_ref(*rows):
+        return cot_v.at[ALONG_X, b_rows(*rows)]
+
+    def b_own():
+        arrived(cot_v.at[ALONG_X, partner_rows], zl_r.at[ALONG_X], zl_s.at[ALONG_X])
+        mine = b_ref(0, 0)
+        start(remote(mine, mine, xr_s.at[ALONG_X, 0], fl_r.at[ALONG_X, 0], right))
+        start(remote(mine, mine, xl_s.at[ALONG_X, 0], fr_r.at[ALONG_X, 0], left))
+
+    def b_forward():
+        arrived(b_ref(0, 1), fl_r.at[ALONG_X, 0], xr_s.at[ALONG_X, 0])
+        arrived(b_ref(0, 2), fr_r.at[ALONG_X, 0], xl_s.at[ALONG_X, 0])
+        for n, device in ((1, right), (2, left)):
+            half = b_ref(0, n, 32 * (n - 1), 32)
+            start(remote(half, half, xf_s.at[ALONG_X, n], xf_r.at[ALONG_X, n], device))
+
+    def b_y(n):
+        if n == 3:
+            for m in (1, 2):
+                arrived(b_ref(0, 3, 32 * (m - 1), 32), xf_r.at[ALONG_X, m], xf_s.at[ALONG_X, m])
+        for j in (1, 3, 2):
+            start(remote(b_ref(0, n), b_ref(back(j), n), by_s.at[n, j], by_r.at[n, back(j)],
+                         plane(0, j)))
+
+    def b_done():
+        for n in range(4):
+            for j in (1, 3, 2):
+                arrived(b_ref(j, n), by_r.at[n, j], by_s.at[n, j])
+
     steps = dict(
+        bown=b_own, bfwd=b_forward, by=b_y, bdone=b_done,
         ysend=y_sends, own=own, fwd=forward, done=done, wsend=w_sends, farr=far_ready, wown=w_own,
         wnear=w_near, wfar=w_far, woth=w_other, home=home, hsend=hidden_sends,
         harr=hidden_arrived, term=term, tsend=term_sends, gadd=grad_add, ladd=last_add,
@@ -407,12 +454,12 @@
         pltpu.VMEM((TOK, HID), BF16),
         pltpu.VMEM((TOK, HID), BF16),
         pltpu.VMEM((HID, SHARD), F32),
-        dma(8), dma(4), dma(4), dma(4, 4), dma(4, 4),
+        dma(10), dma(4), dma(4), dma(4, 4), dma(4, 4),
         dma(4, 4), dma(4, 4), dma(4, 4), dma(4, 4), dma(4, 4), dma(4, 4),
         dma(4, 4), dma(4, 4), dma(4, 4), dma(4, 4),
         dma(4), dma(4), dma(4), dma(4),
-        dma(4), dma(4), dma(2), dma(2), dma(4), dma(4), dma(4), dma(4),
-        dma(4), dma(4), dma(8),
+        dma(4), dma(4), dma(2), dma(2), dma(3, 2), dma(3, 2), dma(4), dma(4),
+        dma(4), dma(4), dma(4, 4), dma(4, 4), dma(8),
         pltpu.SemaphoreType.REGULAR,
     ]
     return pl.pallas_call(
@@ -434,28 +481,50 @@
     )(gate_pre, up_pre, cotangent, w_prev)
 
 
-def body(gate_pre, up_pre, cotangent, w_prev, param_next, grad_next, moment_one, moment_two):
-    gate_grad, up_grad, grad_prev = grads(gate_pre, up_pre, cotangent, w_prev)
-    moment_one_f = beta_first * moment_one.astype(jnp.float32) + (1.0 - beta_first) * grad_next
-    moment_two_f = (
-        beta_second * moment_two.astype(jnp.float32) + (1.0 - beta_second) * grad_next * grad_next
-    )
+def finish_kernel(
+    gg, ug, gp, param, grad, one, two, gg_out, ug_out, gp_out, param_out, one_out, two_out, step_out
+):
+    gg_out[...] = gg[...]
+    ug_out[...] = ug[...]
+    gp_out[...] = gp[...]
+    g = grad[...]
+    moment_one_f = beta_first * one[...].astype(F32) + (1.0 - beta_first) * g
+    moment_two_f = beta_second * two[...].astype(F32) + (1.0 - beta_second) * g * g
     first_fix = 1.0 - beta_first**STEP
     second_fix = 1.0 - beta_second**STEP
     adam_step = (
         moment_one_f / first_fix / (jnp.sqrt(moment_two_f / second_fix) + epsilon)
-        + decay_rate * param_next
+        + decay_rate * param[...]
     )
-    param_new = param_next - learn_rate * adam_step
-    return (
-        gate_grad,
-        up_grad,
-        grad_prev,
-        param_new,
-        moment_one_f.astype(jnp.bfloat16),
-        moment_two_f.astype(jnp.bfloat16),
-        adam_step,
-    )
+    param_out[...] = param[...] - learn_rate * adam_step
+    one_out[...] = moment_one_f.astype(BF16)
+    two_out[...] = moment_two_f.astype(BF16)
+    step_out[...] = adam_step
+
+
+def finish(gate_grad, up_grad, grad_prev, param_next, grad_next, moment_one, moment_two):
+    parts = 2
+    tokens = pl.BlockSpec((TOK // parts, HID), lambda i: (i, 0))
+    part = pl.BlockSpec((HID // parts, SHARD), lambda i: (i, 0))
+
+    def like(*arrays):
+        return tuple(jax.ShapeDtypeStruct(a.shape, a.dtype) for a in arrays)
+
+    return pl.pallas_call(
+        finish_kernel,
+        grid=(parts,),
+        out_shape=like(gate_grad, up_grad, grad_prev, param_next, moment_one, moment_two, param_next),
+        in_specs=[tokens] * 2 + [part] * 5,
+        out_specs=(tokens,) * 2 + (part,) * 5,
+        cost_estimate=pl.CostEstimate(
+            flops=20 * HID * SHARD, bytes_accessed=12 * 2**20, transcendentals=2 * HID * SHARD
+        ),
+    )(gate_grad, up_grad, grad_prev, param_next, grad_next, moment_one, moment_two)
+
+
+def body(gate_pre, up_pre, cotangent, w_prev, param_next, grad_next, moment_one, moment_two):
+    partial = grads(gate_pre, up_pre, cotangent, w_prev)
+    return finish(*partial, param_next, grad_next, moment_one, moment_two)
 
 
 def solution(mesh):

time: 110 us -> 97.6 us (0.89); the launches traced: 110 us -> 96.6 us
  Pallas kernels: 102 us -> 95.9 us
  local copies, waits for them, and re-layouts: 3.95 us -> 0 us
  other arithmetic: 3.81 us -> 0 us
    pallas_call x1, Pallas kernels: 102 us -> 91.2 us  [grads(): pl.pallas_call(kernel, out_shape=(jax.ShapeDtypeStruct((TOK, HID), BF16),...]
    pallas_call x0 -> x1, Pallas kernels: none -> 4.69 us  [finish(): pl.pallas_call(finish_kernel, grid=(parts,), out_shape=like(gate_grad, up...]
    unnamed x13 -> x0, local copies, waits for them, and re-layouts: 3.95 us -> none
    sub x1 -> x0, other arithmetic: 3.81 us -> none  [body(): param_new = param_next - learn_rate * adam_step]
where the time goes in v3:
time: 97.6 us; the launch traced here: 96.6 us
  Pallas kernels  95.9 us (98%)
    pallas_call x1, Pallas kernels, grads(): pl.pallas_call(kernel, out_shape=(jax.ShapeDtypeStruct((TOK, HID), BF16),...  91.2 us
    pallas_call x1, Pallas kernels, finish(): pl.pallas_call(finish_kernel, grid=(parts,), out_shape=like(gate_grad, up...  4.69 us

profile of v3, /device:TPU:1, one launch (start us, length us, event | category | flops | bytes accessed | tf_op | source)
XLA Modules:
  0.0 96.6 jit_solution(6770213763297582035)
XLA Ops:
  0.6 91.2 %shard_map.135 = (bf16[256,1792]{1,0:T(8,128)(2,1)}, bf16[256,1792]{1,0:T(8,128)(2,1)}, f32[1792,128]{1,0:T(8,128)}) custom-call(bf16[256,1792]{1,0:T(8,128)(2,1)} %gate_ref.1, bf16[256,1792]{1,0:T(8,128)(2,1)} %up_ref.1, bf16[32,4096]{1,0:T(8,128)(2,1)} %cot_ref.1, bf16[1792,128]{1,0:T(8,128)(2,1)} %w_ref.1), custom_call_target="tpu_custom_call" | custom-call | flops 7516192768 | bytes 8388608 | tf_op jit(solution)/shard_map/pallas_call | solution.py:465
  91.9 4.7 %shard_map.136 = (bf16[256,1792]{1,0:T(8,128)(2,1)}, bf16[256,1792]{1,0:T(8,128)(2,1)}, f32[1792,128]{1,0:T(8,128)}, f32[1792,128]{1,0:T(8,128)}, bf16[1792,128]...) custom-call(bf16[256,1792]{1,0:T(8,128)(2,1)} %get-tuple-element.10.gg, ...), custom_call_target="tpu_custom_call" | custom-call | flops 4587520 | bytes 12582912 | tf_op jit(solution)/shard_map/pallas_call | solution.py:513

commit v4 on v3

--- a/solution.py
+++ b/solution.py
@@ -35,7 +35,7 @@
     ("own", 3, 2), ("done", 1, 0), ("done", 1, 1), ("term", 1), ("own", 3, 0), ("own", 3, 1),
     ("by", 3), ("tsend", 1), ("fwd", 3, 2), ("gadd", 1), ("fwd", 3, 3), ("wfar",), ("bdone",),
     ("term", 2), ("done", 3, 3), ("ladd", 3), ("fwd", 3, 0), ("fwd", 3, 1), ("woth", 0),
-    ("gadd", 2), ("done", 3, 2), ("tsend", 2), ("gadd", 0), ("gsend", 2), ("gsend", 3),
+    ("tsend", 2), ("gadd", 2), ("done", 3, 2), ("gadd", 0), ("gsend", 2), ("gsend", 3),
     ("ladd", 2), ("done", 3, 0), ("done", 3, 1), ("ladd", 1), ("gsend", 1), ("lterms",),
     ("lsends",), ("gsend", 0), ("gres",), ("pres",),
 )

time: 97.6 us -> 98 us (level)
  Pallas kernels: 95.9 us -> 97 us
    pallas_call x1, Pallas kernels: 91.2 us -> 92.3 us  [grads(): pl.pallas_call(kernel, out_shape=(jax.ShapeDtypeStruct((TOK, HID), BF16),...]
where the time goes in v4:
time: 98 us; the launch traced here: 97.6 us
  Pallas kernels  97 us (99%)
    pallas_call x1, Pallas kernels, grads(): pl.pallas_call(kernel, out_shape=(jax.ShapeDtypeStruct((TOK, HID), BF16),...  92.3 us
    pallas_call x1, Pallas kernels, finish(): pl.pallas_call(finish_kernel, grid=(parts,), out_shape=like(gate_grad, up...  4.69 us

profile of v4, /device:TPU:1, one launch (start us, length us, event | category | flops | bytes accessed | tf_op | source)
XLA Modules:
  0.0 97.6 jit_solution(4993744517762616936)
XLA Ops:
  0.6 92.3 %shard_map.135 = (bf16[256,1792]{1,0:T(8,128)(2,1)}, bf16[256,1792]{1,0:T(8,128)(2,1)}, f32[1792,128]{1,0:T(8,128)}) custom-call(bf16[256,1792]{1,0:T(8,128)(2,1)} %gate_ref.1, bf16[256,1792]{1,0:T(8,128)(2,1)} %up_ref.1, bf16[32,4096]{1,0:T(8,128)(2,1)} %cot_ref.1, bf16[1792,128]{1,0:T(8,128)(2,1)} %w_ref.1), custom_call_target="tpu_custom_call" | custom-call | flops 7516192768 | bytes 8388608 | tf_op jit(solution)/shard_map/pallas_call | solution.py:465
  92.9 4.7 %shard_map.136 = (bf16[256,1792]{1,0:T(8,128)(2,1)}, bf16[256,1792]{1,0:T(8,128)(2,1)}, f32[1792,128]{1,0:T(8,128)}, f32[1792,128]{1,0:T(8,128)}, bf16[1792,128]...) custom-call(bf16[256,1792]{1,0:T(8,128)(2,1)} %get-tuple-element.10.gg, ...), custom_call_target="tpu_custom_call" | custom-call | flops 4587520 | bytes 12582912 | tf_op jit(solution)/shard_map/pallas_call | solution.py:513
